TPU v7x, 32 devices: a whole 2x2x4 slice. The times are simulated.
32 devices in a mesh: col: 4 (over y, x), row: 2 (over core), leaf: 4 (over z).
Axes of the slice: x: 2, y: 2, z: 4, core: 2. Of those that a mesh axis runs over, the one named last changes fastest.
Arguments:
- rhs_top: float32 [4, 4, 32, 1024], P(None, 'col', None, 'row'), may hold values from -6 to 6
- diag_inv: bfloat16 [4, 4, 1024, 1024], P(None, 'col', 'row'), may hold values from -1 to 1.25, as said below
- tile_vals: bfloat16 [4, 4, 2, 8, 4, 128, 128], P(None, 'col', None, 'row'), may hold values from -0.1875 to 0.1875
- tile_pattern: int32 [4, 4, 2, 8, 4], P(None, 'col', None, 'row'), may hold values from 0 to 7, as said below
- sub_vals: bfloat16 [4, 4, 2, 8, 4, 128, 128], P('col', 'leaf', None, 'row'), may hold values from -0.1875 to 0.1875
- sub_pattern: int32 [4, 4, 2, 8, 4], P('col', 'leaf', None, 'row'), may hold values from 0 to 7, as said below
- sub_solved: bfloat16 [4, 4, 32, 1024], P('col', 'leaf'), may hold values from -6 to 6
Outputs:
- solved: float32 [4, 4, 32, 1024], P(None, 'col', None, 'row')
- outgoing: float32 [4, 2, 32, 1024], P('col', None, None, 'row')
Inputs may be any that keep to these rules, and one draw needn't show every extreme that they name: `tile_pattern`: in each row block of a panel tile the 4 column blocks are distinct. `sub_pattern`: in each row block of a subtree tile the 4 column blocks are distinct. `diag_inv`: lower triangular.
All inputs are finite; a program needn't handle non-finite values.
Results may differ from a plain program's by a relative error of at most 0.012.
Values may be sent and summed in bfloat16 or wider, within the bound.
A program may use at most 64 MiB of HBM per device.

v0:
```python
import jax
import jax.numpy as jnp
from jax import lax
from jax.sharding import PartitionSpec as P

STEPS = 4


def from_behind(block, axis, distance):
    devices = range(lax.axis_size(axis))
    route = [((i - distance) % len(devices), i) for i in devices]
    return lax.ppermute(block, axis, route)


def apply_tiles(vectors, values, pattern):
    nrows, width = vectors.shape
    block = values.shape[-1]
    blocks = vectors.reshape(nrows, width // block, block).transpose(1, 0, 2)
    chosen = blocks[pattern]
    result = jnp.einsum("hbkri,hbkij->hrbj", chosen, values, preferred_element_type=jnp.float32)
    return result.reshape(2, nrows, values.shape[1] * block)


def panel_update(rhs_b, inverse, values, pattern):
    whole = lax.all_gather(rhs_b, "row", axis=1, tiled=True)
    full_solved = lax.dot_general(
        whole, inverse, (((1,), (1,)), ((), ())), preferred_element_type=jnp.float32
    )
    width = rhs_b.shape[1]
    solved = lax.dynamic_slice_in_dim(full_solved, lax.axis_index("row") * width, width, 1)
    return (solved, apply_tiles(full_solved.astype(jnp.bfloat16), values, pattern))


def per_device(rhs_top, diag_inv, tile_vals, tile_pattern, sub_vals, sub_pattern, sub_solved):
    inverses = lax.all_gather(diag_inv, "row", axis=2, tiled=True)
    partial_value = apply_tiles(sub_solved[0, 0], sub_vals[0, 0], sub_pattern[0, 0])
    merged = lax.psum(partial_value, "leaf")
    outputs = []
    recv_first = merged[0]
    recv_second = merged[1]
    for level in range(STEPS):
        rhs_b = (rhs_top[level, 0] - recv_first).astype(jnp.bfloat16)
        solved, update = panel_update(
            rhs_b, inverses[level, 0], tile_vals[level, 0], tile_pattern[level, 0]
        )
        outputs.append(solved)
        sending = jnp.stack([update[0] + recv_second, update[1]], axis=0)
        moved = from_behind(sending, "col", 1)
        recv_first = moved[0]
        recv_second = moved[1]
    final_pair = jnp.stack([recv_first, recv_second], axis=0)
    solved_all = jnp.stack(outputs, axis=0)[:, None]
    return (solved_all, final_pair[None])


def solution(mesh):
    placed = (
        P(None, "col", None, "row"),
        P(None, "col", "row", None),
        P(None, "col", None, "row", None, None, None),
        P(None, "col", None, "row", None),
        P("col", "leaf", None, "row", None, None, None),
        P("col", "leaf", None, "row", None),
        P("col", "leaf", None, None),
    )
    return jax.shard_map(
        per_device,
        mesh=mesh,
        in_specs=placed,
        out_specs=(P(None, "col", None, "row"), P("col", None, None, "row")),
        check_vma=False,
    )
```

profile of v0, /device:TPU:0, one launch (start us, length us, event | category | flops | bytes accessed | tf_op | source)
XLA Modules:
  0.0 110.0 jit_solution(16038552596391030463)
XLA Ops:
  8.0 0.0 copy-start
  8.0 0.0 copy-start.3
  8.0 0.0 copy-start.1
  8.0 0.0 all-reduce.2.cloned.1.call-start
  8.1 0.8 compare_select_fusion.4
  8.9 0.1 reshape.186
  9.0 0.9 copy.67
  9.8 0.6 gather_fusion
  10.4 0.0 copy-done
  10.4 0.3 convolution_bitcast_fusion.4
  10.7 0.7 copy.78
  11.4 0.0 all-reduce.2.cloned.1.call-update
  11.4 0.0 all-gather.2.cloned.1.call-start
  11.5 0.5 all-gather.2.cloned.1.call-update
  12.0 0.0 copy-done.3
  12.0 0.1 reshape.194
  12.1 0.1 reshape.210
  12.2 36.8 %all-reduce.2.cloned.1.call-done = f32[2,32,512]{2,1,0:T(8,128)} async-done(((f32[2,32,512]{2,1,0:T(8,128)}), f32[2,32,512]{2,1,0:T(8,128)}) %all-reduce.2.cloned.1.call-update) | async-done | bytes 131088 | tf_op jit(solution)/shard_map/psum | solution.py:37
  49.0 0.0 copy-done.1
  49.0 0.0 copy-start.2
  49.0 0.9 fusion.20
  49.9 1.9 %all_gather.15 = bf16[32,1024]{1,0:T(8,128)(2,1)S(1)} all-gather(bf16[32,512]{1,0:T(8,128)(2,1)S(1)} %fusion.20), channel_id=1, replica_groups=mesh['col'=4,'row'=2,'leaf'=4] {'row'}, dimensions={1}, use_global_device_ids=true | all-gather | bytes 98304 | tf_op jit(solution)/shard_map/all_gather | solution.py:25
  51.7 0.0 all-gather.2.cloned.1.call-done
  51.7 2.3 %fusion.3 = f32[32,1024]{1,0:T(8,128)S(1)} fusion(bf16[32,1024]{1,0:T(8,128)(2,1)S(1)} %all_gather.15, bf16[4,1,1024,1024]{3,2,1,0:T(8,128)(2,1)} %all-gather.2.cloned.1.call-done), kind=kOutput, calls=%fused_computation.12 | convolution fusion | flops 67108864 | bytes 2293760 | tf_op jit(solution)/shard_map/dot_general | solution.py:26
  54.1 0.6 gather_fusion.1
  54.7 1.5 %convolution_bitcast_fusion.3 = f32[2,32,4,128]{3,1,2,0:T(8,128)S(1)} fusion(bf16[2,4,4,32,128]{4,3,2,1,0:T(8,128)(2,1)S(1)} %bitcast.178, bf16[4,1,2,4,4,128,128]{6,5,4,3,2,1,0:T(8,128)(2,1)} %param.9), kind=kOutput, calls=%fused_computation.16 | convolution fusion | flops 33554432 | bytes 1441792 | tf_op jit(solution)/shard_map/hbkri,hbkij->hrbj/dot_general | solution.py:20
  56.3 0.0 copy-done.2
  56.4 1.5 %collective-permute-start = (f32[2,32,512]{2,1,0:T(8,128)S(1)}, f32[2,32,512]{2,1,0:T(8,128)S(1)}, u32[]{:S(2)}, u32[]{:S(2)}) collective-permute-start(f32[2,32,512]{2,1,0:T(8,128)S(1)} %pad_maximum_fusion), channel_id=1, source_target_pairs={{24,0},{0,8},{8,16},{16,24},{25,1},{1,9},{9,17},{17,25},{26,2},{2,... | collective-permute-start | bytes 393224 | tf_op jit(solution)/shard_map/ppermute | solution.py:12
  57.9 0.1 reshape.218
  57.9 0.1 reshape.202
  58.0 4.9 %collective-permute-done = f32[2,32,512]{2,1,0:T(8,128)S(1)} collective-permute-done((f32[2,32,512]{2,1,0:T(8,128)S(1)}, f32[2,32,512]{2,1,0:T(8,128)S(1)}, u32[]{:S(2)}, u32[]{:S(2)}) %collective-permute-start) | collective-permute-done | bytes 131104 | tf_op jit(solution)/shard_map/ppermute | solution.py:12
  62.9 1.9 %all_gather.17 = bf16[32,1024]{1,0:T(8,128)(2,1)S(1)} all-gather(bf16[32,512]{1,0:T(8,128)(2,1)S(1)} %fusion.18), channel_id=1, replica_groups=mesh['col'=4,'row'=2,'leaf'=4] {'row'}, dimensions={1}, use_global_device_ids=true | all-gather | bytes 98304 | tf_op jit(solution)/shard_map/all_gather | solution.py:25
  64.8 2.3 %fusion.2 = f32[32,1024]{1,0:T(8,128)S(1)} fusion(bf16[32,1024]{1,0:T(8,128)(2,1)S(1)} %all_gather.17, bf16[4,1,1024,1024]{3,2,1,0:T(8,128)(2,1)} %all-gather.2.cloned.1.call-done), kind=kOutput, calls=%fused_computation.10 | convolution fusion | flops 67108864 | bytes 2293760 | tf_op jit(solution)/shard_map/dot_general | solution.py:26
  67.1 0.6 gather_fusion.2
  67.7 1.5 %convolution_bitcast_fusion.2 = f32[2,32,4,128]{3,1,2,0:T(8,128)S(1)} fusion(bf16[2,4,4,32,128]{4,3,2,1,0:T(8,128)(2,1)S(1)} %bitcast.179, bf16[4,1,2,4,4,128,128]{6,5,4,3,2,1,0:T(8,128)(2,1)} %param.9), kind=kOutput, calls=%fused_computation.15 | convolution fusion | flops 33554432 | bytes 1441792 | tf_op jit(solution)/shard_map/hbkri,hbkij->hrbj/dot_general | solution.py:20
  69.4 0.6 collective-permute-start.1
  70.0 5.9 %collective-permute-done.1 = f32[2,32,512]{2,1,0:T(8,128)S(1)} collective-permute-done((f32[2,32,512]{2,1,0:T(8,128)S(1)}, f32[2,32,512]{2,1,0:T(8,128)S(1)}, u32[]{:S(2)}, u32[]{:S(2)}) %collective-permute-start.1) | collective-permute-done | bytes 131104 | tf_op jit(solution)/shard_map/ppermute | solution.py:12
  75.9 1.9 %all_gather.18 = bf16[32,1024]{1,0:T(8,128)(2,1)S(1)} all-gather(bf16[32,512]{1,0:T(8,128)(2,1)S(1)} %fusion.16), channel_id=1, replica_groups=mesh['col'=4,'row'=2,'leaf'=4] {'row'}, dimensions={1}, use_global_device_ids=true | all-gather | bytes 98304 | tf_op jit(solution)/shard_map/all_gather | solution.py:25
  77.8 2.3 %fusion.1 = f32[32,1024]{1,0:T(8,128)S(1)} fusion(bf16[32,1024]{1,0:T(8,128)(2,1)S(1)} %all_gather.18, bf16[4,1,1024,1024]{3,2,1,0:T(8,128)(2,1)} %all-gather.2.cloned.1.call-done), kind=kOutput, calls=%fused_computation.8 | convolution fusion | flops 67108864 | bytes 2293760 | tf_op jit(solution)/shard_map/dot_general | solution.py:26
  80.1 0.6 gather_fusion.3
  80.7 1.5 %convolution_bitcast_fusion.1 = f32[2,32,4,128]{3,1,2,0:T(8,128)S(1)} fusion(bf16[2,4,4,32,128]{4,3,2,1,0:T(8,128)(2,1)S(1)} %bitcast.180, bf16[4,1,2,4,4,128,128]{6,5,4,3,2,1,0:T(8,128)(2,1)} %param.9), kind=kOutput, calls=%fused_computation.14 | convolution fusion | flops 33554432 | bytes 1441792 | tf_op jit(solution)/shard_map/hbkri,hbkij->hrbj/dot_general | solution.py:20
  82.4 0.1 collective-permute-start.2
  82.5 6.4 %collective-permute-done.2 = f32[2,32,512]{2,1,0:T(8,128)S(1)} collective-permute-done((f32[2,32,512]{2,1,0:T(8,128)S(1)}, f32[2,32,512]{2,1,0:T(8,128)S(1)}, u32[]{:S(2)}, u32[]{:S(2)}) %collective-permute-start.2) | collective-permute-done | bytes 131104 | tf_op jit(solution)/shard_map/ppermute | solution.py:12
  88.9 1.9 %all_gather.19 = bf16[32,1024]{1,0:T(8,128)(2,1)S(1)} all-gather(bf16[32,512]{1,0:T(8,128)(2,1)S(1)} %fusion.14), channel_id=1, replica_groups=mesh['col'=4,'row'=2,'leaf'=4] {'row'}, dimensions={1}, use_global_device_ids=true | all-gather | bytes 98304 | tf_op jit(solution)/shard_map/all_gather | solution.py:25
  90.8 2.3 %fusion = f32[32,1024]{1,0:T(8,128)S(1)} fusion(bf16[32,1024]{1,0:T(8,128)(2,1)S(1)} %all_gather.19, bf16[4,1,1024,1024]{3,2,1,0:T(8,128)(2,1)} %all-gather.2.cloned.1.call-done), kind=kOutput, calls=%fused_computation.6 | convolution fusion | flops 67108864 | bytes 2293760 | tf_op jit(solution)/shard_map/dot_general | solution.py:26
  93.1 0.6 gather_fusion.4
  93.7 1.5 %convolution_bitcast_fusion = f32[2,32,4,128]{3,1,2,0:T(8,128)S(1)} fusion(bf16[2,4,4,32,128]{4,3,2,1,0:T(8,128)(2,1)S(1)} %bitcast.181, bf16[4,1,2,4,4,128,128]{6,5,4,3,2,1,0:T(8,128)(2,1)} %param.9), kind=kOutput, calls=%fused_computation.13 | convolution fusion | flops 33554432 | bytes 1441792 | tf_op jit(solution)/shard_map/hbkri,hbkij->hrbj/dot_general | solution.py:20
  95.4 0.1 collective-permute-start.3
  95.5 0.7 maximum_bitcast_fusion
  96.2 5.7 %collective-permute-done.3 = f32[2,32,512]{2,1,0:T(8,128)S(1)} collective-permute-done((f32[2,32,512]{2,1,0:T(8,128)S(1)}, f32[2,32,512]{2,1,0:T(8,128)S(1)}, u32[]{:S(2)}, u32[]{:S(2)}) %collective-permute-start.3) | collective-permute-done | bytes 131104 | tf_op jit(solution)/shard_map/ppermute | solution.py:12
  101.9 0.7 copy.82
  (42 shorter events, 0.8 us)
Async XLA Ops:
  8.0 2.4 %copy-start = (bf16[1,1,2,4,4,128,128]{6,5,4,3,2,1,0:T(8,128)(2,1)S(1)}, bf16[1,1,2,4,4,128,128]{6,5,4,3,2,1,0:T(8,128)(2,1)}, u32[]{:S(2)}) copy-start(bf16[1,1,2,4,4,128,128]{6,5,4,3,2,1,0:T(8,128)(2,1)} %param.11) | copy-start | bytes 3145732
  8.0 4.0 %copy-start.3 = (s32[4,1,2,4,4]{4,3,2,1,0:T(4,128)S(1)}, s32[4,1,2,4,4]{4,3,2,1,0:T(4,128)}, u32[]{:S(2)}) copy-start(s32[4,1,2,4,4]{4,3,2,1,0:T(4,128)} %param.10) | copy-start | bytes 1540
  8.0 40.9 %copy-start.1 = (f32[4,1,32,512]{3,2,1,0:T(8,128)S(1)}, f32[4,1,32,512]{3,2,1,0:T(8,128)}, u32[]{:S(2)}) copy-start(f32[4,1,32,512]{3,2,1,0:T(8,128)} %param.7) | copy-start | bytes 786436
  8.0 40.9 %all-reduce.2.cloned.1.call-start = ((), (), s32[]{:S(2)}) async-start(), calls=%async_computation | async-start | bytes 262144 | tf_op jit(solution)/shard_map/psum | solution.py:37
  11.4 40.3 %all-gather.2.cloned.1.call-start = ((), (), s32[]{:S(2)}) async-start(), calls=%async_computation.1 | async-start | bytes 12582912 | tf_op jit(solution)/shard_map/all_gather | solution.py:35
  49.0 7.4 %copy-start.2 = (f32[2,32,512]{2,1,0:T(8,128)S(1)}, f32[2,32,512]{2,1,0:T(8,128)}, u32[]{:S(2)}) copy-start(f32[2,32,512]{2,1,0:T(8,128)} %all-reduce.2.cloned.1.call-done) | copy-start | bytes 393220
  56.4 6.5 %collective-permute-start = (f32[2,32,512]{2,1,0:T(8,128)S(1)}, f32[2,32,512]{2,1,0:T(8,128)S(1)}, u32[]{:S(2)}, u32[]{:S(2)}) collective-permute-start(f32[2,32,512]{2,1,0:T(8,128)S(1)} %pad_maximum_fusion), channel_id=1, source_target_pairs={{24,0},{0,8},{8,16},{16,24},{25,1},{1,9},{9,17},{17,25},{26,2},{2,... | collective-permute-start | bytes 393224 | tf_op jit(solution)/shard_map/ppermute | solution.py:12
  69.4 6.5 %collective-permute-start.1 = (f32[2,32,512]{2,1,0:T(8,128)S(1)}, f32[2,32,512]{2,1,0:T(8,128)S(1)}, u32[]{:S(2)}, u32[]{:S(2)}) collective-permute-start(f32[2,32,512]{2,1,0:T(8,128)S(1)} %pad_maximum_fusion.1), channel_id=1, source_target_pairs={{24,0},{0,8},{8,16},{16,24},{25,1},{1,9},{9,17},{17,25},{26,2},{2,... | collective-permute-start | bytes 393224 | tf_op jit(solution)/shard_map/ppermute | solution.py:12
  82.4 6.5 %collective-permute-start.2 = (f32[2,32,512]{2,1,0:T(8,128)S(1)}, f32[2,32,512]{2,1,0:T(8,128)S(1)}, u32[]{:S(2)}, u32[]{:S(2)}) collective-permute-start(f32[2,32,512]{2,1,0:T(8,128)S(1)} %pad_maximum_fusion.2), channel_id=1, source_target_pairs={{24,0},{0,8},{8,16},{16,24},{25,1},{1,9},{9,17},{17,25},{26,2},{2,... | collective-permute-start | bytes 393224 | tf_op jit(solution)/shard_map/ppermute | solution.py:12
  95.4 6.5 %collective-permute-start.3 = (f32[2,32,512]{2,1,0:T(8,128)S(1)}, f32[2,32,512]{2,1,0:T(8,128)S(1)}, u32[]{:S(2)}, u32[]{:S(2)}) collective-permute-start(f32[2,32,512]{2,1,0:T(8,128)S(1)} %pad_maximum_fusion.3), channel_id=1, source_target_pairs={{24,0},{0,8},{8,16},{16,24},{25,1},{1,9},{9,17},{17,25},{26,2},{2,... | collective-permute-start | bytes 393224 | tf_op jit(solution)/shard_map/ppermute | solution.py:12
Sparse Core Ops, SparseCore 0:
  11.8 37.1 all-reduce.1
Sparse Core Ops, SparseCore 1:
  13.5 22.4 all-gather.1
where the time goes:
time: 111 us; the launch traced here: 110 us
  waiting for transfers between devices  60.2 us (54%)
  between operations  15.9 us (14%)
  matrix products  15.5 us (14%)
  blocking collectives  7.41 us (7%)
  local copies, waits for them, and re-layouts  6.12 us (6%)
  other arithmetic  2.69 us (2%)
  starting transfers between devices  2.24 us (2%)
    psum x1, waiting for transfers between devices, per_device(): merged = lax.psum(partial_value, 'leaf')  36.8 us
    ppermute x4, waiting for transfers between devices, from_behind(): return lax.ppermute(block, axis, route)  22.9 us
    dot_general x4, matrix products, panel_update(): lax.dot_general(whole, inverse, (((1,), (1,)), ((), ())), preferred_eleme...  9.21 us
    all_gather x4, blocking collectives, panel_update(): whole = lax.all_gather(rhs_b, 'row', axis=1, tiled=True)  7.41 us
    dot_general x5, matrix products, apply_tiles(): jnp.einsum('hbkri,hbkij->hrbj', chosen, values, preferred_element_type=jn...  6.28 us
    gather x5, local copies, waits for them, and re-layouts, apply_tiles(): chosen = blocks[pattern]  3.01 us
  transfers between devices with their start and end apart: 6, of which 5 were waited for; matrix products, arithmetic and copies ran while one was open for 2% of the time, Pallas kernels for 0%

commit v1 on v0

v1 whole, which is shorter than its diff:
```python
import functools

import jax
import jax.numpy as jnp
from jax import lax
from jax.experimental import pallas as pl
from jax.experimental.pallas import tpu as pltpu
from jax.sharding import PartitionSpec as P

MESH = pl.DeviceIdType.MESH
F32 = jnp.float32
BF16 = jnp.bfloat16


def pack(x):
    half = x.shape[1] // 2
    return jnp.concatenate([x[:, :half], x[:, half:]], axis=0)


def kernel(
    sizes,
    rhs_hbm,
    diag_hbm,
    tile_hbm,
    tile_pat,
    sub_hbm,
    sub_pat,
    subx_hbm,
    solved_out,
    outgoing,
    subv,
    subx,
    subx3,
    tiles,
    diag,
    rhs0,
    rhsn,
    part_send,
    part0,
    part1,
    xmsg,
    xsend,
    cmsg,
    csend,
    sx3,
    sol,
    fin,
    load_sem,
    send_sem,
    part0_sem,
    part1_sem,
    diag_sem,
    rhs_sem,
    x_sem,
    c_sem,
    sol_sem,
    fin_sem,
):
    C, R, L, G, S, NRHS, W, BLK, NBR, NB = sizes
    m = NRHS // G
    c, r, l = lax.axis_index("col"), lax.axis_index("row"), lax.axis_index("leaf")
    g = lax.rem(l, G)
    base = l - g
    nxt, prv = lax.rem(c + 1, C), lax.rem(c + C - 1, C)
    rows = pl.ds(pl.multiple_of(g * m, m), m)
    started = []

    def leaf_at(d):
        return lax.rem(l + d, L)

    def row_at(d):
        return lax.rem(r + d, R)

    def mate(d):
        return base + lax.rem(g + d, G)

    loads = []

    def load(src, dst):
        copy = pltpu.make_async_copy(src, dst, load_sem.at[len(loads)])
        copy.start()
        loads.append(copy)
        return copy

    def send(src, dst, sem, target):
        copy = pltpu.make_async_remote_copy(
            src_ref=src,
            dst_ref=dst,
            send_sem=send_sem.at[len(started)],
            recv_sem=sem,
            device_id=target,
            device_id_type=MESH,
        )
        copy.start()
        started.append(copy)

    def arrived(dst, sem):
        pltpu.make_async_remote_copy(
            src_ref=dst,
            dst_ref=dst,
            send_sem=send_sem.at[0],
            recv_sem=sem,
            device_id=(c, r, l),
            device_id_type=MESH,
        ).wait_recv()

    barrier = pltpu.get_barrier_semaphore()
    peers = []
    for dl in range(L):
        for dr in range(R):
            if dl or dr:
                peers.append((c, row_at(dr), leaf_at(dl)))
    for other in (nxt, prv):
        for dr in range(R):
            peers.append((other, row_at(dr), l))
        for d in range(1, G):
            peers.append((other, r, mate(d)))
    for peer in peers:
        pl.semaphore_signal(barrier, inc=1, device_id=peer, device_id_type=MESH)

    load_x = load(subx_hbm.at[0, 0], subx)
    load_v = load(sub_hbm.at[0, 0], subv)
    load_r = load(rhs_hbm.at[0, 0, rows], rhs0.at[r])
    load_d, load_t = [], []
    for s in range(S):
        load_d.append(load(diag_hbm.at[s, 0], diag.at[s, r]))
        load_t.append(load(tile_hbm.at[s, 0], tiles.at[s]))

    pl.semaphore_wait(barrier, len(peers))

    for dr in range(1, R):
        send(rhs_hbm.at[0, 0, rows], rhs0.at[r], rhs_sem.at[r], (c, row_at(dr), l))
        send(diag_hbm.at[0, 0], diag.at[0, r], diag_sem.at[0, r], (c, row_at(dr), l))
    send(rhs_hbm.at[pl.ds(1, S - 1), 0, rows], rhsn, rhs_sem.at[R], (prv, r, l))

    def product(lookup, pat, vals):
        lhs = jnp.concatenate([lookup(pat(k)) for k in range(NB)], axis=1)
        return jnp.dot(lhs.astype(BF16), vals[...].reshape(NB * BLK, BLK), preferred_element_type=F32)

    load_x.wait()
    for k in range(subx3.shape[0]):
        subx3[k] = subx[:, k * BLK : (k + 1) * BLK]
    load_v.wait()
    for h in range(2):
        part = jnp.concatenate(
            [
                product(lambda i: subx3[i], lambda k: sub_pat[0, 0, h, b, k], subv.at[h, b])
                for b in range(NBR)
            ],
            axis=1,
        )
        for j in range(G):
            part_send[h, j] = pack(part[j * m : (j + 1) * m]).astype(BF16)
        if h == 0:
            part0[l, r] = part_send[0, g]
            for dl in range(L):
                for dr in range(R):
                    if dl or dr:
                        there = leaf_at(dl)
                        send(
                            part_send.at[0, lax.rem(there, G)],
                            part0.at[l, r],
                            part0_sem.at[l, r],
                            (c, row_at(dr), there),
                        )
        else:
            part1[l] = part_send[1, g]
            for dl in range(1, L):
                there = leaf_at(dl)
                send(part_send.at[1, lax.rem(there, G)], part1.at[l], part1_sem.at[l], (c, r, there))
    for s in range(1, S):
        for dr in range(1, R):
            send(diag_hbm.at[s, 0], diag.at[s, r], diag_sem.at[s, r], (c, row_at(dr), l))

    load_r.wait()
    for dr in range(1, R):
        there = row_at(dr)
        arrived(rhs0.at[there], rhs_sem.at[there])
    for dl in range(L):
        for dr in range(R):
            if dl or dr:
                i, j = leaf_at(dl), row_at(dr)
                arrived(part0.at[i, j], part0_sem.at[i, j])
    pieces = []
    for j in range(R):
        total = part0[0, j].astype(F32)
        for i in range(1, L):
            total = total + part0[i, j].astype(F32)
        value = pack(rhs0[j]) - total
        pieces += [value[:m], value[m:]]

    for s in range(S):
        if s > 0:
            pieces = []
            for j in range(R):
                arrived(xmsg.at[s - 1, j], x_sem.at[s - 1, j])
                value = xmsg[s - 1, j].astype(F32)
                pieces += [value[:m], value[m:]]
        x = jnp.concatenate(pieces, axis=1).astype(BF16)
        load_d[s].wait()
        for dr in range(1, R):
            there = row_at(dr)
            arrived(diag.at[s, there], diag_sem.at[s, there])
        step = W // 2
        for i in range(2 * R):
            reach = (i + 1) * step
            block = lax.dot_general(
                x[:, :reach],
                diag[s, i // 2, (i % 2) * step : (i % 2 + 1) * step, :reach],
                (((1,), (1,)), ((), ())),
                preferred_element_type=F32,
            )
            sol[s, i // 2, :, (i % 2) * step : (i % 2 + 1) * step] = block
            for k in range(step // BLK):
                sx3[s, i * (step // BLK) + k] = block[:, k * BLK : (k + 1) * BLK]

        load_t[s].wait()

        def update(h):
            return jnp.concatenate(
                [
                    product(lambda i: sx3[s, i], lambda k: tile_pat[s, 0, h, b, k], tiles.at[s, h, b])
                    for b in range(NBR)
                ],
                axis=1,
            )

        def carried():
            if s > 0:
                arrived(cmsg.at[s - 1], c_sem.at[s - 1])
                return cmsg[s - 1]
            for dl in range(1, L):
                i = leaf_at(dl)
                arrived(part1.at[i], part1_sem.at[i])
            total = part1[0].astype(F32)
            for i in range(1, L):
                total = total + part1[i].astype(F32)
            return jnp.concatenate([total[:m], total[m:]], axis=1)

        if s < S - 1:
            if s == 0:
                arrived(rhsn, rhs_sem.at[R])
            first = rhsn[s] - (update(0) + carried())
            xsend[s] = pack(first).astype(BF16)
            for dr in range(R):
                send(xsend.at[s], xmsg.at[s, r], x_sem.at[s, r], (nxt, row_at(dr), l))
            csend[s] = update(1)
            send(csend.at[s], cmsg.at[s], c_sem.at[s], (nxt, r, l))
        load(sol.at[s, r], solved_out.at[s, 0, rows])
        for d in range(1, G):
            send(sol.at[s, r], solved_out.at[s, 0, rows], sol_sem.at[s, g], (c, r, mate(d)))
        if s == S - 1:
            for h in range(2):
                fin[h] = update(h) + carried() if h == 0 else update(h)
                for d in range(G):
                    send(fin.at[h], outgoing.at[0, h, rows], fin_sem.at[h, g], (nxt, r, mate(d)))

    for s in range(S):
        for d in range(1, G):
            j = lax.rem(g + d, G)
            there = pl.ds(pl.multiple_of(j * m, m), m)
            arrived(solved_out.at[s, 0, there], sol_sem.at[s, j])
    for h in range(2):
        for j in range(G):
            arrived(outgoing.at[0, h, pl.ds(j * m, m)], fin_sem.at[h, j])
    for copy in loads[-S:]:
        copy.wait()
    for copy in started:
        copy.wait_send()


def per_device(axes, rhs_top, diag_inv, tile_vals, tile_pattern, sub_vals, sub_pattern, sub_solved):
    C, R, L = axes
    S, _, NRHS, W = rhs_top.shape
    NBR, NB, BLK = tile_vals.shape[3:6]
    PW = diag_inv.shape[3]
    SW = sub_solved.shape[3]
    G = max(1, min(L, NRHS // 8))
    m = NRHS // G
    sizes = (C, R, L, G, S, NRHS, W, BLK, NBR, NB)
    hbm = pl.BlockSpec(memory_space=pltpu.HBM)
    out = pl.BlockSpec(memory_space=pl.ANY)
    smem = pl.BlockSpec(memory_space=pltpu.SMEM)
    dma = pltpu.SemaphoreType.DMA
    n_sends = (
        2 * (R - 1) + 1 + (L * R - 1) + (L - 1) + (S - 1) * (R - 1) + (S - 1) * (R + 1) + S * (G - 1) + 2 * G
    )
    return pl.pallas_call(
        functools.partial(kernel, sizes),
        out_shape=(
            jax.ShapeDtypeStruct((S, 1, NRHS, W), F32),
            jax.ShapeDtypeStruct((1, 2, NRHS, W), F32),
        ),
        in_specs=[hbm, hbm, hbm, smem, hbm, smem, hbm],
        out_specs=(out, out),
        scratch_shapes=[
            pltpu.VMEM(sub_vals.shape[2:], BF16),
            pltpu.VMEM((NRHS, SW), BF16),
            pltpu.VMEM((SW // BLK, NRHS, BLK), BF16),
            pltpu.VMEM((S,) + tile_vals.shape[2:], BF16),
            pltpu.VMEM((S, R, W, PW), BF16),
            pltpu.VMEM((R, m, W), F32),
            pltpu.VMEM((S - 1, m, W), F32),
            pltpu.VMEM((2, G, 2 * m, W // 2), BF16),
            pltpu.VMEM((L, R, 2 * m, W // 2), BF16),
            pltpu.VMEM((L, 2 * m, W // 2), BF16),
            pltpu.VMEM((S - 1, R, 2 * m, W // 2), BF16),
            pltpu.VMEM((S - 1, 2 * m, W // 2), BF16),
            pltpu.VMEM((S - 1, m, W), F32),
            pltpu.VMEM((S - 1, m, W), F32),
            pltpu.VMEM((S, PW // BLK, m, BLK), F32),
            pltpu.VMEM((S, R, m, W), F32),
            pltpu.VMEM((2, m, W), F32),
            dma((3 + 3 * S,)),
            dma((n_sends,)),
            dma((L, R)),
            dma((L,)),
            dma((S, R)),
            dma((R + 1,)),
            dma((S - 1, R)),
            dma((S - 1,)),
            dma((S, G)),
            dma((2, G)),
        ],
        compiler_params=pltpu.CompilerParams(
            collective_id=0, has_side_effects=True, vmem_limit_bytes=48 * 1024 * 1024
        ),
    )(rhs_top, diag_inv, tile_vals, tile_pattern, sub_vals, sub_pattern, sub_solved)


def solution(mesh):
    placed = (
        P(None, "col", None, "row"),
        P(None, "col", "row", None),
        P(None, "col", None, "row", None, None, None),
        P(None, "col", None, "row", None),
        P("col", "leaf", None, "row", None, None, None),
        P("col", "leaf", None, "row", None),
        P("col", "leaf", None, None),
    )
    axes = tuple(mesh.shape[name] for name in ("col", "row", "leaf"))
    return jax.shard_map(
        functools.partial(per_device, axes),
        mesh=mesh,
        in_specs=placed,
        out_specs=(P(None, "col", None, "row"), P("col", None, None, "row")),
        check_vma=False,
    )
```

time: 111 us -> 40 us (0.36)
  waiting for transfers between devices: 60.2 us -> 0 us
  Pallas kernels: 0 us -> 31 us
  matrix products: 15.5 us -> 0 us
  between operations: 15.9 us -> 0.65 us
  blocking collectives: 7.41 us -> 0 us
  other arithmetic: 2.69 us -> 0 us
  starting transfers between devices: 2.24 us -> 0 us
  local copies, waits for them, and re-layouts: 6.12 us -> 7.96 us
    psum x1 -> x0, waiting for transfers between devices: 36.8 us -> none  [per_device(): merged = lax.psum(partial_value, 'leaf')]
    pallas_call x0 -> x1, Pallas kernels: none -> 31 us  [per_device(): pl.pallas_call(functools.partial(kernel, sizes), out_shape=(jax.ShapeDtyp...]
    ppermute x4 -> x0, waiting for transfers between devices: 22.9 us -> none  [from_behind(): return lax.ppermute(block, axis, route)]
    dot_general x9 -> x0, matrix products: 15.5 us -> none  [the longest x4 9.21 us: panel_update(): lax.dot_general(whole, inverse, (((1,), (1,)), ((), ())), preferred_eleme...]
    all_gather x4 -> x0, blocking collectives: 7.41 us -> none  [panel_update(): whole = lax.all_gather(rhs_b, 'row', axis=1, tiled=True)]
    unnamed x10 -> x14, local copies, waits for them, and re-layouts: 1.53 us -> 7.96 us
    gather x5 -> x0, local copies, waits for them, and re-layouts: 3.01 us -> none  [apply_tiles(): chosen = blocks[pattern]]
    ppermute x4 -> x0, starting transfers between devices: 2.16 us -> none  [from_behind(): return lax.ppermute(block, axis, route)]
  transfers between devices with their start and end apart: 6 -> 0, of which waited for: 5 -> 0; matrix products, arithmetic and copies ran while one was open for 2% -> 0% of each run, Pallas kernels for 0% -> 0%
where the time goes in v1:
time: 40 us; the launch traced here: 39.6 us
  Pallas kernels  31 us (78%)
  local copies, waits for them, and re-layouts  7.96 us (20%)
  between operations  0.65 us (2%)
    pallas_call x1, Pallas kernels, per_device(): pl.pallas_call(functools.partial(kernel, sizes), out_shape=(jax.ShapeDtyp...  31 us
    unnamed x14, local copies, waits for them, and re-layouts  7.96 us

profile of v1, /device:TPU:0, one launch (start us, length us, event | category | flops | bytes accessed | tf_op | source)
XLA Modules:
  0.0 39.6 jit_solution(15481440947978281897)
XLA Ops:
  0.6 0.0 copy-start
  0.6 2.2 %copy-done = bf16[4,1,512,1024]{3,2,1,0:T(8,128)(2,1)S(1)} copy-done((bf16[4,1,512,1024]{3,2,1,0:T(8,128)(2,1)S(1)}, bf16[4,1,512,1024]{3,2,1,0:T(8,128)(2,1)}, u32[]{:S(2)}) %copy-start) | copy-done | bytes 4194328
  2.8 0.0 copy-start.1
  2.8 1.2 %copy-done.1 = bf16[1,1,2,4,4,128,128]{6,5,4,3,2,1,0:T(8,128)(2,1)S(1)} copy-done((bf16[1,1,2,4,4,128,128]{6,5,4,3,2,1,0:T(8,128)(2,1)S(1)}, bf16[1,1,2,4,4,128,128]{6,5,4,3,2,1,0:T(8,128)(2,1)}, u32[]{:S(2)}) %copy-start.1) | copy-done | bytes 1048600
  4.0 0.0 copy-start.2
  4.0 0.9 %copy-done.2 = f32[4,1,32,512]{3,2,1,0:T(8,128)S(1)} copy-done((f32[4,1,32,512]{3,2,1,0:T(8,128)S(1)}, f32[4,1,32,512]{3,2,1,0:T(8,128)}, u32[]{:S(2)}) %copy-start.2) | copy-done | bytes 262168
  5.0 0.0 copy-start.3
  5.0 0.8 %copy-done.3 = bf16[1,1,32,1024]{3,2,1,0:T(8,128)(2,1)S(1)} copy-done((bf16[1,1,32,1024]{3,2,1,0:T(8,128)(2,1)S(1)}, bf16[1,1,32,1024]{3,2,1,0:T(8,128)(2,1)}, u32[]{:S(2)}) %copy-start.3) | copy-done | bytes 65560
  5.8 0.0 copy-start.4
  5.8 0.7 %copy-done.4 = s32[4,1,2,4,4]{4,3,2,1,0:T(4,128)S(1)} copy-done((s32[4,1,2,4,4]{4,3,2,1,0:T(4,128)S(1)}, s32[4,1,2,4,4]{4,3,2,1,0:T(4,128)}, u32[]{:S(2)}) %copy-start.4) | copy-done | bytes 536
  6.6 0.0 copy-start.5
  6.6 0.7 %copy-done.5 = s32[1,1,2,4,4]{4,3,2,1,0:T(4,128)S(1)} copy-done((s32[1,1,2,4,4]{4,3,2,1,0:T(4,128)S(1)}, s32[1,1,2,4,4]{4,3,2,1,0:T(4,128)}, u32[]{:S(2)}) %copy-start.5) | copy-done | bytes 152
  7.2 31.0 %shard_map.86 = (f32[4,1,32,512]{3,2,1,0:T(8,128)S(1)}, f32[1,2,32,512]{3,2,1,0:T(8,128)S(1)}) custom-call(f32[4,1,32,512]{3,2,1,0:T(8,128)S(1)} %copy-done.2, bf16[4,1,512,1024]{3,2,1,0:T(8,128)(2,1)S(1)} %copy-done, bf16[4,1,2,4,4,128,128]{6,5,4,3,2,1,0:T(8,128)(2,1)} %tile_hbm.1, s32[4,1,2,4,4]{4,3,2,1,0:T(4,128)S(1)} %copy-done.4, ...), custom_call_target="tpu_custom_call" | custom-call | tf_op jit(solution)/shard_map/pallas_call | solution.py:288
  38.3 0.7 %copy.11 = f32[4,1,32,512]{3,2,1,0:T(8,128)} copy(f32[4,1,32,512]{3,2,1,0:T(8,128)S(1)} %get-tuple-element.4) | data formatting | bytes 524288
  39.0 0.7 %copy.12 = f32[1,2,32,512]{3,2,1,0:T(8,128)} copy(f32[1,2,32,512]{3,2,1,0:T(8,128)S(1)} %get-tuple-element.5) | data formatting | bytes 262144
Async XLA Ops:
  0.6 2.2 %copy-start = (bf16[4,1,512,1024]{3,2,1,0:T(8,128)(2,1)S(1)}, bf16[4,1,512,1024]{3,2,1,0:T(8,128)(2,1)}, u32[]{:S(2)}) copy-start(bf16[4,1,512,1024]{3,2,1,0:T(8,128)(2,1)} %diag_hbm.1) | copy-start | bytes 12582916
  2.8 1.2 %copy-start.1 = (bf16[1,1,2,4,4,128,128]{6,5,4,3,2,1,0:T(8,128)(2,1)S(1)}, bf16[1,1,2,4,4,128,128]{6,5,4,3,2,1,0:T(8,128)(2,1)}, u32[]{:S(2)}) copy-start(bf16[1,1,2,4,4,128,128]{6,5,4,3,2,1,0:T(8,128)(2,1)} %sub_hbm.1) | copy-start | bytes 3145732
  4.0 0.9 %copy-start.2 = (f32[4,1,32,512]{3,2,1,0:T(8,128)S(1)}, f32[4,1,32,512]{3,2,1,0:T(8,128)}, u32[]{:S(2)}) copy-start(f32[4,1,32,512]{3,2,1,0:T(8,128)} %rhs_hbm.1) | copy-start | bytes 786436
  5.0 0.8 %copy-start.3 = (bf16[1,1,32,1024]{3,2,1,0:T(8,128)(2,1)S(1)}, bf16[1,1,32,1024]{3,2,1,0:T(8,128)(2,1)}, u32[]{:S(2)}) copy-start(bf16[1,1,32,1024]{3,2,1,0:T(8,128)(2,1)} %subx_hbm.1) | copy-start | bytes 196612
  5.8 0.7 %copy-start.4 = (s32[4,1,2,4,4]{4,3,2,1,0:T(4,128)S(1)}, s32[4,1,2,4,4]{4,3,2,1,0:T(4,128)}, u32[]{:S(2)}) copy-start(s32[4,1,2,4,4]{4,3,2,1,0:T(4,128)} %tile_pat.1) | copy-start | bytes 1540
  6.6 0.7 %copy-start.5 = (s32[1,1,2,4,4]{4,3,2,1,0:T(4,128)S(1)}, s32[1,1,2,4,4]{4,3,2,1,0:T(4,128)}, u32[]{:S(2)}) copy-start(s32[1,1,2,4,4]{4,3,2,1,0:T(4,128)} %sub_pat.1) | copy-start | bytes 388

commit v2 on v1

--- a/solution.py
+++ b/solution.py
@@ -26,8 +26,8 @@
     sub_hbm,
     sub_pat,
     subx_hbm,
-    solved_out,
-    outgoing,
+    solved_all,
+    fin_all,
     subv,
     subx,
     subx3,
@@ -113,8 +113,6 @@
     for other in (nxt, prv):
         for dr in range(R):
             peers.append((other, row_at(dr), l))
-        for d in range(1, G):
-            peers.append((other, r, mate(d)))
     for peer in peers:
         pl.semaphore_signal(barrier, inc=1, device_id=peer, device_id_type=MESH)
 
@@ -125,13 +123,6 @@
     for s in range(S):
         load_d.append(load(diag_hbm.at[s, 0], diag.at[s, r]))
         load_t.append(load(tile_hbm.at[s, 0], tiles.at[s]))
-
-    pl.semaphore_wait(barrier, len(peers))
-
-    for dr in range(1, R):
-        send(rhs_hbm.at[0, 0, rows], rhs0.at[r], rhs_sem.at[r], (c, row_at(dr), l))
-        send(diag_hbm.at[0, 0], diag.at[0, r], diag_sem.at[0, r], (c, row_at(dr), l))
-    send(rhs_hbm.at[pl.ds(1, S - 1), 0, rows], rhsn, rhs_sem.at[R], (prv, r, l))
 
     def product(lookup, pat, vals):
         lhs = jnp.concatenate([lookup(pat(k)) for k in range(NB)], axis=1)
@@ -151,23 +142,29 @@
         )
         for j in range(G):
             part_send[h, j] = pack(part[j * m : (j + 1) * m]).astype(BF16)
-        if h == 0:
-            part0[l, r] = part_send[0, g]
-            for dl in range(L):
-                for dr in range(R):
-                    if dl or dr:
-                        there = leaf_at(dl)
-                        send(
-                            part_send.at[0, lax.rem(there, G)],
-                            part0.at[l, r],
-                            part0_sem.at[l, r],
-                            (c, row_at(dr), there),
-                        )
-        else:
-            part1[l] = part_send[1, g]
-            for dl in range(1, L):
+    part0[l, r] = part_send[0, g]
+    part1[l] = part_send[1, g]
+
+    pl.semaphore_wait(barrier, len(peers))
+
+    for dr in range(1, R):
+        send(rhs_hbm.at[0, 0, rows], rhs0.at[r], rhs_sem.at[r], (c, row_at(dr), l))
+    for dl in range(L):
+        for dr in range(R):
+            if dl or dr:
                 there = leaf_at(dl)
-                send(part_send.at[1, lax.rem(there, G)], part1.at[l], part1_sem.at[l], (c, r, there))
+                send(
+                    part_send.at[0, lax.rem(there, G)],
+                    part0.at[l, r],
+                    part0_sem.at[l, r],
+                    (c, row_at(dr), there),
+                )
+    for dr in range(1, R):
+        send(diag_hbm.at[0, 0], diag.at[0, r], diag_sem.at[0, r], (c, row_at(dr), l))
+    for dl in range(1, L):
+        there = leaf_at(dl)
+        send(part_send.at[1, lax.rem(there, G)], part1.at[l], part1_sem.at[l], (c, r, there))
+    send(rhs_hbm.at[pl.ds(1, S - 1), 0, rows], rhsn, rhs_sem.at[R], (prv, r, l))
     for s in range(1, S):
         for dr in range(1, R):
             send(diag_hbm.at[s, 0], diag.at[s, r], diag_sem.at[s, r], (c, row_at(dr), l))
@@ -246,27 +243,38 @@
                 send(xsend.at[s], xmsg.at[s, r], x_sem.at[s, r], (nxt, row_at(dr), l))
             csend[s] = update(1)
             send(csend.at[s], cmsg.at[s], c_sem.at[s], (nxt, r, l))
-        load(sol.at[s, r], solved_out.at[s, 0, rows])
+        solved_all[s, g] = pack(sol[s, r]).astype(BF16)
         for d in range(1, G):
-            send(sol.at[s, r], solved_out.at[s, 0, rows], sol_sem.at[s, g], (c, r, mate(d)))
+            send(solved_all.at[s, g], solved_all.at[s, g], sol_sem.at[s, g], (c, r, mate(d)))
         if s == S - 1:
             for h in range(2):
-                fin[h] = update(h) + carried() if h == 0 else update(h)
+                fin[h] = pack(update(h) + carried() if h == 0 else update(h)).astype(BF16)
                 for d in range(G):
-                    send(fin.at[h], outgoing.at[0, h, rows], fin_sem.at[h, g], (nxt, r, mate(d)))
+                    send(fin.at[h], fin_all.at[h, g], fin_sem.at[h, g], (nxt, r, mate(d)))
 
     for s in range(S):
         for d in range(1, G):
             j = lax.rem(g + d, G)
-            there = pl.ds(pl.multiple_of(j * m, m), m)
-            arrived(solved_out.at[s, 0, there], sol_sem.at[s, j])
+            arrived(solved_all.at[s, j], sol_sem.at[s, j])
     for h in range(2):
         for j in range(G):
-            arrived(outgoing.at[0, h, pl.ds(j * m, m)], fin_sem.at[h, j])
-    for copy in loads[-S:]:
-        copy.wait()
+            arrived(fin_all.at[h, j], fin_sem.at[h, j])
     for copy in started:
         copy.wait_send()
+
+
+def unpack_kernel(m, solved_all, fin_all, solved_out, outgoing):
+    half = solved_all.shape[3]
+    for i in range(solved_all.shape[0]):
+        for j in range(solved_all.shape[1]):
+            value = solved_all[i, j].astype(F32)
+            solved_out[i, 0, j * m : (j + 1) * m, :half] = value[:m]
+            solved_out[i, 0, j * m : (j + 1) * m, half:] = value[m:]
+    for i in range(fin_all.shape[0]):
+        for j in range(fin_all.shape[1]):
+            value = fin_all[i, j].astype(F32)
+            outgoing[0, i, j * m : (j + 1) * m, :half] = value[:m]
+            outgoing[0, i, j * m : (j + 1) * m, half:] = value[m:]
 
 
 def per_device(axes, rhs_top, diag_inv, tile_vals, tile_pattern, sub_vals, sub_pattern, sub_solved):
@@ -279,17 +287,17 @@
     m = NRHS // G
     sizes = (C, R, L, G, S, NRHS, W, BLK, NBR, NB)
     hbm = pl.BlockSpec(memory_space=pltpu.HBM)
-    out = pl.BlockSpec(memory_space=pl.ANY)
+    out = pl.BlockSpec(memory_space=pltpu.VMEM)
     smem = pl.BlockSpec(memory_space=pltpu.SMEM)
     dma = pltpu.SemaphoreType.DMA
     n_sends = (
         2 * (R - 1) + 1 + (L * R - 1) + (L - 1) + (S - 1) * (R - 1) + (S - 1) * (R + 1) + S * (G - 1) + 2 * G
     )
-    return pl.pallas_call(
+    solved_all, fin_all = pl.pallas_call(
         functools.partial(kernel, sizes),
         out_shape=(
-            jax.ShapeDtypeStruct((S, 1, NRHS, W), F32),
-            jax.ShapeDtypeStruct((1, 2, NRHS, W), F32),
+            jax.ShapeDtypeStruct((S, G, 2 * m, W // 2), BF16),
+            jax.ShapeDtypeStruct((2, G, 2 * m, W // 2), BF16),
         ),
         in_specs=[hbm, hbm, hbm, smem, hbm, smem, hbm],
         out_specs=(out, out),
@@ -310,8 +318,8 @@
             pltpu.VMEM((S - 1, m, W), F32),
             pltpu.VMEM((S, PW // BLK, m, BLK), F32),
             pltpu.VMEM((S, R, m, W), F32),
-            pltpu.VMEM((2, m, W), F32),
-            dma((3 + 3 * S,)),
+            pltpu.VMEM((2, 2 * m, W // 2), BF16),
+            dma((3 + 2 * S,)),
             dma((n_sends,)),
             dma((L, R)),
             dma((L,)),
@@ -323,9 +331,18 @@
             dma((2, G)),
         ],
         compiler_params=pltpu.CompilerParams(
-            collective_id=0, has_side_effects=True, vmem_limit_bytes=48 * 1024 * 1024
+            collective_id=0, has_side_effects=True, vmem_limit_bytes=56 * 1024 * 1024
         ),
     )(rhs_top, diag_inv, tile_vals, tile_pattern, sub_vals, sub_pattern, sub_solved)
+    return pl.pallas_call(
+        functools.partial(unpack_kernel, m),
+        out_shape=(
+            jax.ShapeDtypeStruct((S, 1, NRHS, W), F32),
+            jax.ShapeDtypeStruct((1, 2, NRHS, W), F32),
+        ),
+        in_specs=[pl.BlockSpec(memory_space=pltpu.VMEM)] * 2,
+        out_specs=(pl.BlockSpec(memory_space=pltpu.VMEM),) * 2,
+    )(solved_all, fin_all)
 
 
 def solution(mesh):

time: 40 us -> 31.1 us (0.78)
  local copies, waits for them, and re-layouts: 7.96 us -> 0 us
  Pallas kernels: 31 us -> 30.2 us
    unnamed x14 -> x0, local copies, waits for them, and re-layouts: 7.96 us -> none
    pallas_call x1, Pallas kernels: 31 us -> 28.5 us  [per_device(): pl.pallas_call(functools.partial(kernel, sizes), out_shape=(jax.ShapeDtyp...]
    pallas_call x0 -> x1, Pallas kernels: none -> 1.67 us  [per_device(): pl.pallas_call(functools.partial(unpack_kernel, m), out_shape=(jax.ShapeD...]
where the time goes in v2:
time: 31.1 us; the launch traced here: 30.8 us
  Pallas kernels  30.2 us (97%)
  between operations  0.64 us (2%)
    pallas_call x1, Pallas kernels, per_device(): pl.pallas_call(functools.partial(kernel, sizes), out_shape=(jax.ShapeDtyp...  28.5 us
    pallas_call x1, Pallas kernels, per_device(): pl.pallas_call(functools.partial(unpack_kernel, m), out_shape=(jax.ShapeD...  1.67 us

profile of v2, /device:TPU:0, one launch (start us, length us, event | category | flops | bytes accessed | tf_op | source)
XLA Modules:
  0.0 30.8 jit_solution(11103607232152737387)
XLA Ops:
  0.6 28.5 %shard_map.86 = (bf16[4,4,16,256]{3,2,1,0:T(8,128)(2,1)}, bf16[2,4,16,256]{3,2,1,0:T(8,128)(2,1)}) custom-call(f32[4,1,32,512]{3,2,1,0:T(8,128)} %rhs_hbm.1, bf16[4,1,512,1024]{3,2,1,0:T(8,128)(2,1)} %diag_hbm.1, bf16[4,1,2,4,4,128,128]{6,5,4,3,2,1,0:T(8,128)(2,1)} %tile_hbm.1, s32[4,1,2,4,4]{4,3,2,1,0:T(4,128)} %tile_pat.1, ...), custom_call_target="tpu_custom_call" | custom-call | tf_op jit(solution)/shard_map/pallas_call | solution.py:296
  29.2 1.7 %shard_map.87 = (f32[4,1,32,512]{3,2,1,0:T(8,128)}, f32[1,2,32,512]{3,2,1,0:T(8,128)}) custom-call(bf16[4,4,16,256]{3,2,1,0:T(8,128)(2,1)} %get-tuple-element.4.solved_all, bf16[2,4,16,256]{3,2,1,0:T(8,128)(2,1)} %get-tuple-element.5.fin_all), custom_call_target="tpu_custom_call" | custom-call | tf_op jit(solution)/shard_map/pallas_call | solution.py:337

commit v3 on v2

--- a/solution.py
+++ b/solution.py
@@ -45,6 +45,7 @@
     sx3,
     sol,
     fin,
+    mine,
     load_sem,
     send_sem,
     part0_sem,
@@ -225,7 +226,8 @@
         def carried():
             if s > 0:
                 arrived(cmsg.at[s - 1], c_sem.at[s - 1])
-                return cmsg[s - 1]
+                v = cmsg[s - 1].astype(F32)
+                return jnp.concatenate([v[:m], v[m:]], axis=1)
             for dl in range(1, L):
                 i = leaf_at(dl)
                 arrived(part1.at[i], part1_sem.at[i])
@@ -241,11 +243,12 @@
             xsend[s] = pack(first).astype(BF16)
             for dr in range(R):
                 send(xsend.at[s], xmsg.at[s, r], x_sem.at[s, r], (nxt, row_at(dr), l))
-            csend[s] = update(1)
+            csend[s] = pack(update(1)).astype(BF16)
             send(csend.at[s], cmsg.at[s], c_sem.at[s], (nxt, r, l))
-        solved_all[s, g] = pack(sol[s, r]).astype(BF16)
+        mine[s] = pack(sol[s, r]).astype(BF16)
+        load(mine.at[s], solved_all.at[s, g])
         for d in range(1, G):
-            send(solved_all.at[s, g], solved_all.at[s, g], sol_sem.at[s, g], (c, r, mate(d)))
+            send(mine.at[s], solved_all.at[s, g], sol_sem.at[s, g], (c, r, mate(d)))
         if s == S - 1:
             for h in range(2):
                 fin[h] = pack(update(h) + carried() if h == 0 else update(h)).astype(BF16)
@@ -259,6 +262,8 @@
     for h in range(2):
         for j in range(G):
             arrived(fin_all.at[h, j], fin_sem.at[h, j])
+    for copy in loads[-S:]:
+        copy.wait()
     for copy in started:
         copy.wait_send()
 
@@ -287,7 +292,7 @@
     m = NRHS // G
     sizes = (C, R, L, G, S, NRHS, W, BLK, NBR, NB)
     hbm = pl.BlockSpec(memory_space=pltpu.HBM)
-    out = pl.BlockSpec(memory_space=pltpu.VMEM)
+    out = pl.BlockSpec(memory_space=pltpu.HBM)
     smem = pl.BlockSpec(memory_space=pltpu.SMEM)
     dma = pltpu.SemaphoreType.DMA
     n_sends = (
@@ -314,12 +319,13 @@
             pltpu.VMEM((L, 2 * m, W // 2), BF16),
             pltpu.VMEM((S - 1, R, 2 * m, W // 2), BF16),
             pltpu.VMEM((S - 1, 2 * m, W // 2), BF16),
-            pltpu.VMEM((S - 1, m, W), F32),
-            pltpu.VMEM((S - 1, m, W), F32),
+            pltpu.VMEM((S - 1, 2 * m, W // 2), BF16),
+            pltpu.VMEM((S - 1, 2 * m, W // 2), BF16),
             pltpu.VMEM((S, PW // BLK, m, BLK), F32),
             pltpu.VMEM((S, R, m, W), F32),
             pltpu.VMEM((2, 2 * m, W // 2), BF16),
-            dma((3 + 2 * S,)),
+            pltpu.VMEM((S, 2 * m, W // 2), BF16),
+            dma((3 + 3 * S,)),
             dma((n_sends,)),
             dma((L, R)),
             dma((L,)),

time: 31.1 us -> 30.7 us (0.987)
  Pallas kernels: 30.2 us -> 29.8 us
    pallas_call x1, Pallas kernels: 28.5 us -> 28.1 us  [per_device(): pl.pallas_call(functools.partial(kernel, sizes), out_shape=(jax.ShapeDtyp...]
where the time goes in v3:
time: 30.7 us; the launch traced here: 30.4 us
  Pallas kernels  29.8 us (97%)
  between operations  0.64 us (2%)
    pallas_call x1, Pallas kernels, per_device(): pl.pallas_call(functools.partial(kernel, sizes), out_shape=(jax.ShapeDtyp...  28.1 us
    pallas_call x1, Pallas kernels, per_device(): pl.pallas_call(functools.partial(unpack_kernel, m), out_shape=(jax.ShapeD...  1.67 us

profile of v3, /device:TPU:0, one launch (start us, length us, event | category | flops | bytes accessed | tf_op | source)
XLA Modules:
  0.0 30.4 jit_solution(16359303898625197038)
XLA Ops:
  0.6 28.1 %shard_map.86 = (bf16[4,4,16,256]{3,2,1,0:T(8,128)(2,1)}, bf16[2,4,16,256]{3,2,1,0:T(8,128)(2,1)}) custom-call(f32[4,1,32,512]{3,2,1,0:T(8,128)} %rhs_hbm.1, bf16[4,1,512,1024]{3,2,1,0:T(8,128)(2,1)} %diag_hbm.1, bf16[4,1,2,4,4,128,128]{6,5,4,3,2,1,0:T(8,128)(2,1)} %tile_hbm.1, s32[4,1,2,4,4]{4,3,2,1,0:T(4,128)} %tile_pat.1, ...), custom_call_target="tpu_custom_call" | custom-call | tf_op jit(solution)/shard_map/pallas_call | solution.py:301
  28.8 1.7 %shard_map.87 = (f32[4,1,32,512]{3,2,1,0:T(8,128)}, f32[1,2,32,512]{3,2,1,0:T(8,128)}) custom-call(bf16[4,4,16,256]{3,2,1,0:T(8,128)(2,1)} %get-tuple-element.4.solved_all, bf16[2,4,16,256]{3,2,1,0:T(8,128)(2,1)} %get-tuple-element.5.fin_all), custom_call_target="tpu_custom_call" | custom-call | tf_op jit(solution)/shard_map/pallas_call | solution.py:343

commit v4 on v3

--- a/solution.py
+++ b/solution.py
@@ -268,18 +268,34 @@
         copy.wait_send()
 
 
-def unpack_kernel(m, solved_all, fin_all, solved_out, outgoing):
+def unpack_kernel(m, solved_all, fin_all, solved_out, outgoing, packed, packed_fin, plain, plain_fin, sem):
     half = solved_all.shape[3]
-    for i in range(solved_all.shape[0]):
-        for j in range(solved_all.shape[1]):
-            value = solved_all[i, j].astype(F32)
-            solved_out[i, 0, j * m : (j + 1) * m, :half] = value[:m]
-            solved_out[i, 0, j * m : (j + 1) * m, half:] = value[m:]
+    S, G = solved_all.shape[:2]
+    fetch = [
+        pltpu.make_async_copy(fin_all, packed_fin, sem.at[0]),
+        pltpu.make_async_copy(solved_all, packed, sem.at[1]),
+    ]
+    for copy in fetch:
+        copy.start()
+    out = []
+
+    def write(src, i, dst_vmem, dst):
+        for j in range(G):
+            value = src[i, j].astype(F32)
+            dst_vmem[i, j * m : (j + 1) * m, :half] = value[:m]
+            dst_vmem[i, j * m : (j + 1) * m, half:] = value[m:]
+        copy = pltpu.make_async_copy(dst_vmem.at[i], dst, sem.at[2 + len(out)])
+        copy.start()
+        out.append(copy)
+
+    fetch[0].wait()
     for i in range(fin_all.shape[0]):
-        for j in range(fin_all.shape[1]):
-            value = fin_all[i, j].astype(F32)
-            outgoing[0, i, j * m : (j + 1) * m, :half] = value[:m]
-            outgoing[0, i, j * m : (j + 1) * m, half:] = value[m:]
+        write(packed_fin, i, plain_fin, outgoing.at[0, i])
+    fetch[1].wait()
+    for i in range(S):
+        write(packed, i, plain, solved_out.at[i, 0])
+    for copy in out:
+        copy.wait()
 
 
 def per_device(axes, rhs_top, diag_inv, tile_vals, tile_pattern, sub_vals, sub_pattern, sub_solved):
@@ -346,8 +362,15 @@
             jax.ShapeDtypeStruct((S, 1, NRHS, W), F32),
             jax.ShapeDtypeStruct((1, 2, NRHS, W), F32),
         ),
-        in_specs=[pl.BlockSpec(memory_space=pltpu.VMEM)] * 2,
-        out_specs=(pl.BlockSpec(memory_space=pltpu.VMEM),) * 2,
+        in_specs=[hbm] * 2,
+        out_specs=(hbm,) * 2,
+        scratch_shapes=[
+            pltpu.VMEM(solved_all.shape, BF16),
+            pltpu.VMEM(fin_all.shape, BF16),
+            pltpu.VMEM((S, NRHS, W), F32),
+            pltpu.VMEM((2, NRHS, W), F32),
+            dma((S + 4,)),
+        ],
     )(solved_all, fin_all)
 
 

time: 30.7 us -> 30.7 us (level)
  no operation moved by 1% of the time
where the time goes in v4:
time: 30.7 us; the launch traced here: 30.5 us
  Pallas kernels  29.8 us (97%)
  between operations  0.64 us (2%)
    pallas_call x1, Pallas kernels, per_device(): pl.pallas_call(functools.partial(kernel, sizes), out_shape=(jax.ShapeDtyp...  28.1 us
    pallas_call x1, Pallas kernels, per_device(): pl.pallas_call(functools.partial(unpack_kernel, m), out_shape=(jax.ShapeD...  1.71 us

profile of v4, /device:TPU:0, one launch (start us, length us, event | category | flops | bytes accessed | tf_op | source)
XLA Modules:
  0.0 30.5 jit_solution(2803833303092895140)
XLA Ops:
  0.6 28.1 %shard_map.86 = (bf16[4,4,16,256]{3,2,1,0:T(8,128)(2,1)}, bf16[2,4,16,256]{3,2,1,0:T(8,128)(2,1)}) custom-call(f32[4,1,32,512]{3,2,1,0:T(8,128)} %rhs_hbm.1, bf16[4,1,512,1024]{3,2,1,0:T(8,128)(2,1)} %diag_hbm.1, bf16[4,1,2,4,4,128,128]{6,5,4,3,2,1,0:T(8,128)(2,1)} %tile_hbm.1, s32[4,1,2,4,4]{4,3,2,1,0:T(4,128)} %tile_pat.1, ...), custom_call_target="tpu_custom_call" | custom-call | tf_op jit(solution)/shard_map/pallas_call | solution.py:317
  28.8 1.7 %shard_map.87 = (f32[4,1,32,512]{3,2,1,0:T(8,128)}, f32[1,2,32,512]{3,2,1,0:T(8,128)}) custom-call(bf16[4,4,16,256]{3,2,1,0:T(8,128)(2,1)} %get-tuple-element.4.solved_all, bf16[2,4,16,256]{3,2,1,0:T(8,128)(2,1)} %get-tuple-element.5.fin_all), custom_call_target="tpu_custom_call" | custom-call | tf_op jit(solution)/shard_map/pallas_call | solution.py:359
